TPU v7x, 128 devices: a whole 4x4x4 slice. The times are simulated.
128 devices in a mesh: row: 4 (over x), col: 32 (over z, y, core).
Axes of the slice: x: 4, y: 4, z: 4, core: 2. Of those that a mesh axis runs over, the one named last changes fastest.
Arguments:
- sensitivity: bfloat16 [8192, 2, 16384], P('row', None, 'col'), may hold values from -0.25 to 0.25
- sample_weight: float32 [8192], P('row'), may hold values from 0.2 to 5
- pattern: int32 [16, 2, 32], P('row', None, 'col'), may hold values 0 or 1
- prior: float32 [2048], P('row'), may hold values from 0.5 to 5
Outputs:
- factored_band: float32 [2048, 2, 16384], P('row', None, 'col')
Inputs may be any that keep to these rules, and one draw needn't show every extreme that they name: pattern holds only 0 and 1.
All inputs are finite; a program needn't handle non-finite values. No bound on the sum of `pattern` on one device may be relied on, other than what follows from the above.
Results may differ from a plain program's by a relative error of at most 0.0028.
Values may be sent and summed in bfloat16 or wider, within the bound.
A program may use at most 128 MiB of HBM per device.

v0:
```python
import jax
import jax.numpy as jnp
from jax import lax
from jax.sharding import PartitionSpec as P


def spread(value, axis, root):
    mine = lax.axis_index(axis) == root
    return lax.psum(jnp.where(mine, value, jnp.zeros_like(value)), axis)


def body(sensitivity, sample_weight, pattern, prior):
    rows_here = sensitivity.shape[0]
    cycles = sensitivity.shape[1]
    tile = sensitivity.shape[2]
    blocks = pattern.shape[0]
    widths = cycles * tile
    mask_blocks = pattern.astype(jnp.bfloat16)[:, None, :, :]
    masked = (sensitivity.reshape(blocks, tile, cycles, tile) * mask_blocks).reshape(
        rows_here, widths
    )
    weighted = (sample_weight[:, None] * masked.astype(jnp.float32)).astype(jnp.bfloat16)
    first_tile = masked[:, :tile]
    row_count = lax.axis_size("row")
    band_parts = []
    for owner in range(row_count):
        band_parts.append(spread(first_tile, "col", owner))
    band = jnp.concatenate(band_parts, axis=1)
    fisher = lax.psum_scatter(
        jnp.einsum("sb,sc->bc", band, weighted, preferred_element_type=jnp.float32),
        "row",
        scatter_dimension=0,
        tiled=True,
    )
    on_diagonal = (lax.axis_index("col") == lax.axis_index("row")).astype(jnp.float32)
    identity = jnp.eye(tile, dtype=jnp.float32)
    fisher = fisher.at[:, :tile].add(on_diagonal * identity * prior[None, :])
    corner = spread(fisher[:, :tile], "col", 0)
    lower = jnp.linalg.cholesky(corner)
    local_solved = jax.scipy.linalg.solve_triangular(lower, fisher, lower=True)
    solved = spread(local_solved, "row", 0)
    solved_mine = spread(solved[:, :tile], "col", lax.axis_index("row"))
    updated = fisher - jnp.dot(solved_mine.T, solved, precision=lax.Precision.HIGHEST)
    result = jnp.where(lax.axis_index("row") == 0, solved, updated)
    return result.reshape(tile, cycles, tile)


def solution(mesh):
    return jax.shard_map(
        body,
        mesh=mesh,
        in_specs=(P("row", None, "col"), P("row"), P("row", None, "col"), P("row")),
        out_specs=P("row", None, "col"),
        check_vma=False,
    )
```

profile of v0, /device:TPU:71, one launch (start us, length us, event | category | flops | bytes accessed | tf_op | source)
XLA Modules:
  0.0 695.7 jit_solution(14980134706955388091)
XLA Ops:
  6.5 0.7 convert_element_type.13
  7.3 2.2 mul.36
  9.6 1.2 copy.30
  10.8 1.0 copy-done.4
  11.8 1.2 copy.29
  12.9 2.2 mul.38
  15.2 3.5 broadcast_select_fusion.3
  18.7 1.0 copy-done.1
  20.0 122.7 %all-reduce.13.cloned.1.call-done = (bf16[2048,512]{1,0:T(8,128)(2,1)}, bf16[2048,512]{1,0:T(8,128)(2,1)}, bf16[2048,512]{1,0:T(8,128)(2,1)}, bf16[2048,512]{1,0:T(8,128)(2,1)}) async-done(((bf16[2048,512]{1,0:T(8,128)(2,1)}, bf16[2048,512]{1,0:T(8,128)(2,1)}, bf16[2048,512]{1,0:T(8,128)(2,1)}, bf16[2048,512]{1,0:T(8,128)(2,1)}), (bf16[2048,512]{1,0:T(8,128)(2,1)}, bf16[2048,512]{1,0:T(8,128)(2,1)}, ...) | async-done | bytes 8388624 | tf_op jit(solution)/shard_map/psum | solution.py:9
  142.7 15.7 %fusion = f32[2048,1024]{0,1:T(8,128)} fusion(bf16[2048,512]{1,0:T(8,128)(2,1)} %get-tuple-element.37, bf16[2048,512]{1,0:T(8,128)(2,1)} %get-tuple-element.38, bf16[2048,512]{1,0:T(8,128)(2,1)} %get-tuple-element.39, bf16[2048,512]{1,0:T(8,128)(2,1)} %get-tuple-element.40, bf16[2048,1024]{1,0:T(8,128)(2,1)} %copy-done.1, f32[2048]{0:T(1024)S(1)} %copy-done.8), kind=kOutput, calls=%fused_computation.2 | convolution fusion | flops 8629780480 | bytes 20979712 | tf_op jit(solution)/shard_map/sb,sc->bc/dot_general | solution.py:30
  158.5 0.7 compare_reduce_fusion.4
  159.2 77.7 %reduce-scatter.2.cloned.1.call-done = f32[512,1024]{0,1:T(8,128)} async-done(((f32[2048,1024]{0,1:T(8,128)}), f32[512,1024]{0,1:T(8,128)}) %reduce-scatter.2.cloned.1.call-update) | async-done | bytes 2097168 | tf_op jit(solution)/shard_map/reduce_scatter | solution.py:29
  236.9 3.5 fusion.23
  240.4 0.3 all-reduce.9.cloned.1.call-start
  240.7 105.8 %all-reduce.7.cloned.1.call-done = f32[512,512]{0,1:T(8,128)} async-done(((f32[512,512]{0,1:T(8,128)}), f32[512,512]{0,1:T(8,128)}) %all-reduce.7.cloned.1.call-update) | async-done | bytes 1048592 | tf_op jit(solution)/shard_map/psum | solution.py:9
  346.5 1.6 copy.7
  348.4 11.7 %cholesky.103 = f32[128,128]{1,0:T(8,128)S(1)} custom-call(f32[128,128]{1,0:T(8,128)S(1)} %cholesky.263), custom_call_target="Cholesky" | custom-call | tf_op jit(solution)/shard_map/jit(cholesky)/cholesky | solution.py:39
  360.2 9.8 %custom-call.31 = f32[1,128,128]{1,2,0:T(8,128)S(1)} custom-call(f32[1,128,128]{2,1,0:T(8,128)S(1)} %get-tuple-element.54), custom_call_target="InvertDiagBlocksLowerTriangular" | custom-call | tf_op jit(solution)/shard_map/jit(cholesky)/cholesky | solution.py:39
  370.0 0.3 fusion.29
  370.3 0.3 convolution_subtract_fusion.2
  370.6 11.7 %cholesky.215 = f32[128,128]{1,0:T(8,128)S(1)} custom-call(f32[128,128]{1,0:T(8,128)S(1)} %cholesky.267), custom_call_target="Cholesky" | custom-call | tf_op jit(solution)/shard_map/jit(cholesky)/cholesky | solution.py:39
  382.7 10.2 %custom-call.32 = f32[1,128,128]{1,2,0:T(8,128)S(1)} custom-call(f32[1,128,128]{2,1,0:T(8,128)S(1)} %get-tuple-element.52), custom_call_target="InvertDiagBlocksLowerTriangular" | custom-call | tf_op jit(solution)/shard_map/jit(cholesky)/cholesky | solution.py:39
  393.1 0.3 convolution_dynamic-update-slice_fusion
  393.4 1.5 convolution_subtract_fusion.3
  394.9 11.7 %cholesky.236 = f32[128,128]{1,0:T(8,128)S(1)} custom-call(f32[128,128]{1,0:T(8,128)S(1)} %cholesky.272), custom_call_target="Cholesky" | custom-call | tf_op jit(solution)/shard_map/jit(cholesky)/cholesky | solution.py:39
  406.8 9.8 %custom-call.33 = f32[1,128,128]{1,2,0:T(8,128)S(1)} custom-call(f32[1,128,128]{2,1,0:T(8,128)S(1)} %get-tuple-element.50), custom_call_target="InvertDiagBlocksLowerTriangular" | custom-call | tf_op jit(solution)/shard_map/jit(cholesky)/cholesky | solution.py:39
  416.6 0.3 convolution_dynamic-update-slice_fusion.1
  416.9 1.3 convolution_subtract_fusion.4
  418.2 11.9 %cholesky.253 = f32[128,128]{1,0:T(8,128)S(1)} custom-call(f32[128,128]{1,0:T(8,128)S(1)} %convolution_subtract_fusion.4), custom_call_target="Cholesky" | custom-call | tf_op jit(solution)/shard_map/jit(cholesky)/cholesky | solution.py:39
  430.2 0.7 compare_reduce_fusion.1
  431.0 0.6 compare_reduce_fusion
  431.6 0.7 compare_reduce_fusion.2
  434.8 1.1 select_select_fusion
  435.9 14.5 %while.2 = (s32[]{:T(128)}, f32[512,512]{0,1:T(8,128)}, s32[4,2]{0,1:T(2,128)S(1)}, f32[4,128,128]{2,1,0:T(8,128)}, s32[]{:T(128)}) while((s32[]{:T(128)}, f32[512,512]{0,1:T(8,128)}, s32[4,2]{0,1:T(2,128)S(1)}, f32[4,128,128]{2,1,0:T(8,128)}, s32[]{:T(128)}) %tuple.32), condition=%wide.while_cond.1, body=%wide.while_body.1.sunk | while | flops 2 | bytes 393829 | solution.py:40
  436.0 0.6 fusion.55
  436.6 2.2 dynamic-slice.15
  438.9 0.6 bitcast_dynamic-update-slice_fusion.2
  439.6 0.6 fusion.55
  440.2 2.2 dynamic-slice.15
  442.6 0.6 bitcast_dynamic-update-slice_fusion.2
  443.3 0.6 fusion.55
  443.9 2.2 dynamic-slice.15
  446.2 0.6 bitcast_dynamic-update-slice_fusion.2
  446.9 0.6 fusion.55
  447.5 2.2 dynamic-slice.15
  449.8 0.6 bitcast_dynamic-update-slice_fusion.2
  450.5 40.1 %custom-call.34 = f32[4,128,128]{1,2,0:T(8,128)S(1)} custom-call(f32[4,128,128]{2,1,0:T(8,128)} %get-tuple-element.24), custom_call_target="InvertDiagBlocksLowerTriangular" | custom-call | tf_op jit(solution)/shard_map/jit(_solve_triangular)/triangular_solve | solution.py:40
  490.6 0.6 fusion.24
  491.2 1.8 convolution_subtract_fusion.1
  493.1 0.6 fusion.37
  493.7 2.7 convolution_subtract_fusion
  496.5 0.6 fusion.35
  497.1 0.8 copy-done.2
  497.9 4.4 fusion.15
  502.3 2.0 copy.18
  504.3 1.0 copy.17
  505.3 1.0 copy.16
  506.4 1.6 fusion.34
  508.0 2.7 maximum_select_fusion
  511.0 57.0 %all-reduce.9.cloned.1.call-done = f32[512,1024]{0,1:T(8,128)} async-done(((f32[512,1024]{0,1:T(8,128)}), f32[512,1024]{0,1:T(8,128)}) %all-reduce.9.cloned.1.call-update) | async-done | bytes 2097168 | tf_op jit(solution)/shard_map/psum | solution.py:9
  568.0 2.3 slice_select_fusion
  570.4 107.1 %all-reduce.11.cloned.1.call-done = f32[512,512]{0,1:T(8,128)} async-done(((f32[512,512]{0,1:T(8,128)}), f32[512,512]{0,1:T(8,128)}) %all-reduce.11.cloned.1.call-update) | async-done | bytes 1048592 | tf_op jit(solution)/shard_map/psum | solution.py:9
  677.5 7.4 %subtract_select_fusion = f32[512,1024]{0,1:T(8,128)} fusion(f32[512,1024]{0,1:T(8,128)} %all-reduce.9.cloned.1.call-done, f32[512,1024]{0,1:T(8,128)S(1)} %copy-done, f32[512,512]{0,1:T(8,128)} %all-reduce.11.cloned.1.call-done, pred[]{:T(512)S(6)} %eq.24), kind=kOutput, calls=%fused_computation.13 | convolution fusion | flops 3222274048 | bytes 7340033 | tf_op jit(solution)/shard_map/dot_general | solution.py:43
  684.9 4.1 copy.21
  (54 shorter events, 2.4 us)
Async XLA Ops:
  6.5 136.1 %all-reduce.13.cloned.1.call-start = ((), (), s32[]{:S(2)}) async-start(), calls=%async_computation.5 | async-start | bytes 16777216 | tf_op jit(solution)/shard_map/psum | solution.py:9
  9.6 2.2 copy-start.4
  15.2 4.6 copy-start.1
  19.7 122.9 %copy-start.8 = (f32[2048]{0:T(1024)S(1)}, f32[2048]{0:T(1024)}, u32[]{:S(2)}) copy-start(f32[2048]{0:T(1024)} %param.7) | copy-start | bytes 24580
  19.8 217.1 %reduce-scatter.2.cloned.1.call-start = ((), (), s32[]{:S(2)}) async-start(), calls=%async_computation.1 | async-start | bytes 10485760 | tf_op jit(solution)/shard_map/reduce_scatter | solution.py:29
  158.4 78.5 %copy-start.7 = (f32[512]{0:T(512)S(1)}, f32[512]{0:T(512)}, u32[]{:S(2)}) copy-start(f32[512]{0:T(512)} %param.9) | copy-start | bytes 6148
  158.4 188.1 %all-reduce.7.cloned.1.call-start = ((), (), s32[]{:S(2)}) async-start(), calls=%async_computation.2 | async-start | bytes 2097152 | tf_op jit(solution)/shard_map/psum | solution.py:9
  240.4 327.6 %all-reduce.9.cloned.1.call-start = ((), (), s32[]{:S(2)}) async-start(), calls=%async_computation.3 | async-start | bytes 4194304 | tf_op jit(solution)/shard_map/psum | solution.py:9
  346.5 1.7 copy-start.3
  348.4 34.4 %copy-start.5 = (f32[512,512]{1,0:T(8,128)}, f32[512,512]{1,0:T(8,128)S(1)}, u32[]{:S(2)}) copy-start(f32[512,512]{1,0:T(8,128)S(1)} %fusion.21) | copy-start | bytes 3145732
  434.8 55.8 %copy-start = (f32[512,1024]{0,1:T(8,128)S(1)}, f32[512,1024]{0,1:T(8,128)}, u32[]{:S(2)}) copy-start(f32[512,1024]{0,1:T(8,128)} %get-tuple-element.48) | copy-start | bytes 6291460
  497.1 0.8 copy-start.2
  505.3 2.6 copy-start.6
  510.7 166.7 %all-reduce.11.cloned.1.call-start = ((), (), s32[]{:S(2)}) async-start(), calls=%async_computation.4 | async-start | bytes 2097152 | tf_op jit(solution)/shard_map/psum | solution.py:9
Sparse Core Ops, SparseCore 0:
  19.9 122.7 all-reduce.12
  158.5 78.2 reduce-scatter.1
  240.6 105.8 all-reduce.6
  510.9 57.1 all-reduce.8
  571.5 105.9 all-reduce.10
where the time goes:
time: 705 us; the launch traced here: 696 us
  waiting for transfers between devices  470 us (67%)
  other arithmetic  136 us (19%)
  matrix products  39.6 us (6%)
  local copies, waits for them, and re-layouts  32.5 us (5%)
  between operations  16.3 us (2%)
    psum x4, waiting for transfers between devices, spread(): return lax.psum(jnp.where(mine, value, jnp.zeros_like(value)), axis)  393 us
    another operation x14, other arithmetic, body(): lower = jnp.linalg.cholesky(corner)  79 us
    reduce_scatter x1, waiting for transfers between devices, body(): lax.psum_scatter(jnp.einsum('sb,sc->bc', band, weighted, preferred_elemen...  77.7 us
    another operation x3, other arithmetic, body(): local_solved = jax.scipy.linalg.solve_triangular(lower, fisher, lower=True)  41.2 us
    dot_general x1, matrix products, body(): jnp.einsum('sb,sc->bc', band, weighted, preferred_element_type=jnp.float32)  15.7 us
    another operation x20, local copies, waits for them, and re-layouts  14.5 us
  transfers between devices with their start and end apart: 5, of which 5 were waited for; matrix products, arithmetic and copies ran while one was open for 0% of the time, Pallas kernels for 0%

commit v1 on v0

v1 whole, which is shorter than its diff:
```python
import jax
import jax.numpy as jnp
from jax import lax
from jax.experimental import pallas as pl
from jax.experimental.pallas import tpu as pltpu
from jax.sharding import PartitionSpec as P

F32 = jnp.float32
BF16 = jnp.bfloat16
HIGHEST = lax.Precision.HIGHEST
MESH = pl.DeviceIdType.MESH
VMEM = pl.BlockSpec(memory_space=pltpu.VMEM)
NCH = 8
CH = 512 // NCH
SKEW = 3
ON = {'band', 'corner', 'mm', 'rs', 'f0', 'f0r', 'ctree'}
TILES = (0, 2, 1, 3)
T = 4 * NCH + 6 * SKEW
NC = 4
NR = 2
SEND = {
    0: {0: ((0, 3, "mid"), (1, 1, "mid")), 3: ((1, 3, "end"),), 1: ((0, 1, "end"),)},
    2: {0: ((0, 3, "mid"), (1, 1, "mid")), 3: ((1, 3, "end"),), 1: ((0, 1, "end"),)},
    1: {3: ((0, 1, "mid"), (1, 1, "mid")), 2: ((0, 3, "end"), (1, 3, "end"))},
    3: {1: ((0, 3, "mid"), (1, 3, "mid")), 2: ((0, 1, "end"), (1, 1, "end"))},
}
MID = {
    0: {3: ((0, 3),), 1: ((1, 1),)},
    2: {3: ((0, 3),), 1: ((1, 1),)},
    1: {0: ((0, 1), (1, 1))},
    3: {0: ((0, 3), (1, 3))},
}
OWNER = {0: 2, 1: 1, 2: 2, 3: 3}


def dotp(a, b, ca=1, cb=0, precision=None):
    return lax.dot_general(
        a, b, (((ca,), (cb,)), ((), ())), precision=precision, preferred_element_type=F32
    )


def loop(n, f, start=0):
    lax.fori_loop(start, n, lambda i, carry: (f(i), carry)[1], 0)


class Place:
    def __init__(self):
        self.row = lax.axis_index("row")
        self.col = lax.axis_index("col")
        self.core = self.col % 2
        self.y = (self.col // 2) % 4
        self.z = self.col // 8
        self.sib = (self.row, self.col + 1 - 2 * self.core)

    def at(self, z, y, core):
        return (self.row, (z * 4 + y) * 2 + core)

    def along(self, step):
        return ((self.row + step) % 4, self.col)


class Tree:
    def __init__(self, pos, q, sy):
        dz, dy = pos.z, (pos.y - sy + 4) % 4
        mz, my = (4 - dz) % 4, (4 - dy) % 4
        u, v = ((dz, dy), (dy, mz), (mz, my), (my, dz))[q]
        fwd = ((0, 1), (3, 0), (0, 3), (1, 0))[q]
        side = ((1, 0), (0, 1), (3, 0), (0, 3))[q]
        back = tuple((4 - d) % 4 for d in fwd)
        other = tuple((4 - d) % 4 for d in side)
        des = q // 2
        to = lambda d: pos.at((pos.z + d[0]) % 4, (pos.y + d[1]) % 4, des)
        self.at_source = (dz == 0) & (dy == 0)
        self.holder = jnp.logical_not(self.at_source) & (pos.core == des)
        depth = jnp.where(u == 0, v, 2 + jnp.where(u == 2, 1, 0) + jnp.where(v == 0, 1, v - 1))
        depth = jnp.where(pos.core == des, depth, depth + 1)
        self.start = SKEW * jnp.where(self.at_source, 1, depth)
        ahead = ((u == 0) & (v < 3)) | ((u >= 1) & ((v == 1) | (v == 2)))
        turn = tuple(jnp.where(u == 0, a, b) for a, b in zip(side, back))
        self.children = (
            (ahead, to(fwd)),
            (v == 1, to(turn)),
            ((v == 1) & ((u == 0) | (u == 3)), to(other)),
        )
        self.root_child = to(fwd)
        self.sib = pos.sib


def copies_of(tree, src, dst, send, recv, idx):
    out = []
    for n, (pred, to) in enumerate(tree.children + ((True, tree.sib),)):
        out.append((pred, pltpu.make_async_remote_copy(
            src, dst, send.at[(n,) + idx], recv.at[idx], device_id=to, device_id_type=MESH
        )))
    return out


def pass_on(tree, copies, do):
    @pl.when(tree.holder)
    def _():
        for pred, copy in copies[:3]:
            pl.when(pred)(getattr(copy, do))
        getattr(copies[3][1], do)()


def set_out(tree, copies, do):
    getattr(copies[0][1], do)()
    getattr(copies[3][1], do)()


def gather_kernel(
    jt, w0, w1, wrow, prior, f_out, f0_out, f0r_out, corner,
    band, pb, rxm, rxd, f0acc, cpart, crx, dg, dgr,
    b_send, b_recv, own_sem, c_send, c_recv, r_send, r_recv,
    rs_sem, rxm_sem, rxd_sem, f0_send, f0_recv, cx_send, cx_recv, dg_send, dg_recv,
):
    pos = Place()
    r, c = pos.row, pos.col

    barrier = pltpu.get_barrier_semaphore()
    greet = [pos.sib, pos.along(1), pos.along(2), pos.along(3)]
    for core in (0, 1):
        for step in (1, 3):
            greet.append(pos.at((pos.z + step) % 4, pos.y, core))
            greet.append(pos.at(pos.z, (pos.y + step) % 4, core))
    for to in greet:
        pl.semaphore_signal(barrier, inc=1, device_id=to, device_id_type=MESH)
    pl.semaphore_wait(barrier, len(greet))

    chips = [[Tree(pos, q, sy) for q in range(4)] for sy in (0, 1)]

    def band_copies(tree, q, i, own=None):
        src = band.at[q, i] if own is None else jt.at[q, pl.ds(pl.multiple_of(own * CH, CH), CH)]
        return copies_of(tree, src, band.at[q, i], b_send, b_recv, (q, i))

    def band_slot(t):
        for n, tile in enumerate(TILES):
            @pl.when((c == tile) & (t >= NCH * n) & (t < NCH * (n + 1)))
            def _():
                for q in range(4):
                    tree = chips[tile // 2][q]
                    set_out(tree, band_copies(tree, q, t, t - NCH * n), "start")
        for sy in (0, 1):
            for q in range(4):
                tree = chips[sy][q]
                i = t - tree.start - NCH * sy

                @pl.when((i >= 0) & (i < 3 * NCH) & ((i < NCH) | (i >= 2 * NCH)))
                def _():
                    @pl.when(c != 2 * sy + jnp.where(i < NCH, 0, 1))
                    def _():
                        copies = band_copies(tree, q, i + NCH * sy)
                        copies[3][1].wait_recv()
                        pass_on(tree, copies, "start")

    def band_sent():
        for n, tile in enumerate(TILES):
            for q in range(4):
                tree = chips[tile // 2][q]

                def done(ch):
                    copies = band_copies(tree, q, NCH * n + ch)
                    pl.when(c == tile)(lambda: set_out(tree, copies, "wait_send"))
                    pass_on(tree, copies, "wait_send")
                loop(NCH, done)

    def own_tile():
        for n, tile in enumerate(TILES):
            @pl.when(c == tile)
            def _():
                for q in range(4):
                    for ch in range(NCH):
                        band[q, NCH * n + ch] = jt[q, CH * ch:CH * (ch + 1)]

    def corner_x(dst, src, i, kind, frm):
        return pltpu.make_async_remote_copy(
            src, dst, cx_send.at[kind, i - 1], cx_recv.at[kind, frm],
            device_id=pos.along(i), device_id_type=MESH,
        )

    def corner_part():
        @pl.when(c == 0)
        def _():
            a = lax.broadcasted_iota(jnp.int32, (128, 512), 0)
            b = lax.broadcasted_iota(jnp.int32, (128, 512), 1)
            for i in range(4):
                acc = jnp.where((b == a + 128 * i) & (r == 0), prior[...], 0.0)
                for q in range(4):
                    acc += dotp(jt[q, 128 * i:128 * (i + 1), :], w0[q])
                cpart[i] = acc
            for i in (1, 2, 3):
                corner_x(crx.at[r], cpart.at[(r + i) % 4], i, 0, r).start()

    def corner_sum():
        @pl.when(c == 0)
        def _():
            total = cpart[r]
            for i in (1, 2, 3):
                frm = (r + i) % 4
                corner_x(crx.at[frm], crx.at[frm], i, 0, frm).wait_recv()
                total += crx[frm]
            corner[r] = total
            for i in (1, 2, 3):
                corner_x(corner.at[r], corner.at[r], i, 1, r).start()

    def corner_take():
        @pl.when(c == 0)
        def _():
            for i in (1, 2, 3):
                frm = (r + i) % 4
                corner_x(corner.at[frm], corner.at[frm], i, 1, frm).wait_recv()

    def corner_sent():
        @pl.when(c == 0)
        def _():
            for i in (1, 2, 3):
                corner_x(crx.at[r], cpart.at[(r + i) % 4], i, 0, r).wait_send()
                corner_x(corner.at[r], corner.at[r], i, 1, r).wait_send()

    def corner_copies(q, ch):
        n = 128 // NC
        ref = corner.at[q, pl.ds(pl.multiple_of(ch * n, n), n)]
        return copies_of(chips[0][q], ref, ref, c_send, c_recv, (q, ch))

    def corner_slot(t):
        @pl.when((c == 0) & (t < NC))
        def _():
            for q in range(4):
                set_out(chips[0][q], corner_copies(q, t), "start")
        for q in range(4):
            i = t - chips[0][q].start

            @pl.when((c != 0) & (i >= 0) & (i < NC))
            def _():
                copies = corner_copies(q, i)
                copies[3][1].wait_recv()
                pass_on(chips[0][q], copies, "start")

    rtrees = [Tree(pos, q, r // 2) for q in range(4)]

    def f0r_copies(q, ch, own=False):
        n = 128 // NR
        rows = pl.ds(pl.multiple_of(q * 128 + ch * n, n), n)
        src = f0_out.at[0, rows] if own else f0r_out.at[rows]
        return copies_of(rtrees[q], src, f0r_out.at[rows], r_send, r_recv, (q, ch))

    def f0r_slot(t):
        @pl.when((c == r) & (t < NR))
        def _():
            for q in range(4):
                set_out(rtrees[q], f0r_copies(q, t, True), "start")
        for q in range(4):
            i = t - rtrees[q].start

            @pl.when((c != r) & (i >= 0) & (i < NR))
            def _():
                copies = f0r_copies(q, i)
                copies[3][1].wait_recv()
                pass_on(rtrees[q], copies, "start")

    def f0r_own():
        @pl.when(c == r)
        def _():
            f0r_out[...] = f0_out[0]

    def trees_sent():
        for q in range(4):
            for n, at, tree, copies in (
                (NC, 0, chips[0][q], corner_copies), (NR, r, rtrees[q], f0r_copies),
            ):
                if ('ctree' if n == NC else 'f0r') not in ON:
                    continue
                for ch in range(n):
                    cp = copies(q, ch)
                    pl.when(c == at)(lambda: set_out(tree, cp, "wait_send"))
                    pl.when(c != at)(lambda: pass_on(tree, cp, "wait_send"))

    def tile_of(k, q):
        n = TILES.index(k)
        return band[q, NCH * n:NCH * (n + 1)].reshape(512, 512)

    def piece(k, half, n):
        cols = pl.ds(pl.multiple_of(n * 256, 256), 256)
        w = (w0, w1)[half]
        acc = dotp(tile_of(k, 0), w[0, :, cols])
        for q in range(1, 4):
            acc += dotp(tile_of(k, q), w[q, :, cols])
        own = r == OWNER[k]

        def put(value):
            @pl.when(own)
            def _():
                if k == 0:
                    f0acc[half, :, cols] = value
                else:
                    f_out[half, :, cols] = value

            @pl.when(jnp.logical_not(own))
            def _():
                pb[k, half, :, cols] = value.astype(BF16)

        if k == 0 or half == 1:
            put(acc)
            return

        @pl.when(c == 0)
        def _():
            value = acc
            first = pl.ds(pl.multiple_of(n * (NCH // 2), NCH // 2), NCH // 2)
            for q in range(4):
                wk = (tile_of(k, q).astype(F32) * wrow[q]).astype(BF16)
                value = value - dotp(wk, band[q, first].reshape(256, 512), 1, 1)
            put(value)

        @pl.when(c == k)
        def _():
            a = lax.broadcasted_iota(jnp.int32, (512, 256), 0)
            b = lax.broadcasted_iota(jnp.int32, (512, 256), 1)
            on = a == b + n * 256
            line = jnp.sum(jnp.where(on, acc, 0.0), axis=0, keepdims=True)
            dg[:, cols] = jnp.broadcast_to(line, (8, 256))
            put(jnp.where(on, 0.0, acc))

        pl.when((c != 0) & (c != k))(lambda: put(acc))

    def dg_copy(i, frm):
        return pltpu.make_async_remote_copy(
            dg, dgr.at[frm], dg_send, dg_recv.at[frm], device_id=pos.along(i), device_id_type=MESH
        )

    def move(k, half, step, kind):
        e = 0 if k == 0 else 1
        side = 0 if step == 3 else 1
        dst, sem = (
            (rxm.at[k, half], rxm_sem.at[k, half]) if kind == "mid"
            else (rxd.at[e, side, half], rxd_sem.at[e, side, half])
        )
        return pltpu.make_async_remote_copy(
            pb.at[k, half], dst, rs_sem.at[k, half], sem, device_id=pos.along(step), device_id_type=MESH
        )

    def rs_send(k):
        for row, moves in SEND[k].items():
            @pl.when(r == row)
            def _():
                for m in moves:
                    move(k, *m).start()
        if k:
            for i in (1, 2, 3):
                pl.when((c == k) & ((r + i) % 4 == k))(dg_copy(i, r).start)

    def rs_mid(k):
        for row, moves in MID[k].items():
            @pl.when(r == row)
            def _():
                for half, step in moves:
                    move(k, half, step, "mid").wait_recv()
                    pb[k, half] = (pb[k, half].astype(F32) + rxm[k, half].astype(F32)).astype(BF16)
                    move(k, half, step, "end").start()

    def rs_end(k):
        e = 0 if k == 0 else 1

        @pl.when(r == OWNER[k])
        def _():
            for half in (0, 1):
                for step in (1, 3):
                    move(k, half, step, "end").wait_recv()
                got = rxd[e, 0, half].astype(F32) + rxd[e, 1, half].astype(F32)
                if k == 0:
                    f0_out[half] = (f0acc[half] + got).astype(BF16)
                    for step in (1, 3):
                        if 'f0' in ON: f0_copy(half, step).start()
                else:
                    f_out[half] = f_out[half] + got
            if k == 0:
                return

            @pl.when(c == k)
            def _():
                line = prior[...]
                for i in (1, 2, 3):
                    frm = (r + i) % 4
                    dg_copy(i, frm).wait_recv()
                    line = line + dgr[frm, 0:1, :]
                a = lax.broadcasted_iota(jnp.int32, (512, 512), 0)
                b = lax.broadcasted_iota(jnp.int32, (512, 512), 1)
                own = jnp.sum(jnp.where(a == b, f_out[0], 0.0), axis=0, keepdims=True)
                own = own + dg[0:1, :]
                f_out[0] = jnp.where(a == b, own + line, f_out[0])

    def rs_sent(k):
        for table in (SEND, MID):
            for row, moves in table[k].items():
                @pl.when(r == row)
                def _():
                    for m in moves:
                        move(k, m[0], m[1], "end").wait_send()
        if k:
            for i in (1, 2, 3):
                pl.when((c == k) & ((r + i) % 4 == k))(dg_copy(i, r).wait_send)

    def f0_copy(half, step):
        return pltpu.make_async_remote_copy(
            f0_out.at[half], f0_out.at[half], f0_send.at[half, step // 2], f0_recv.at[half],
            device_id=pos.along(step), device_id_type=MESH,
        )

    def f0_pass():
        @pl.when(r != 2)
        def _():
            for half in (0, 1):
                f0_copy(half, 1).wait_recv()
        pl.when(r == 1)(f0_copy(0, 3).start)
        pl.when(r == 3)(f0_copy(1, 1).start)

    def f0_sent():
        @pl.when(r == 2)
        def _():
            for half in (0, 1):
                for step in (1, 3):
                    f0_copy(half, step).wait_send()
        pl.when(r == 1)(f0_copy(0, 3).wait_send)
        pl.when(r == 3)(f0_copy(1, 1).wait_send)

    RS, MM, BA, CO, CT = ('rs' in ON), ('mm' in ON), ('band' in ON), ('corner' in ON), ('ctree' in ON)
    C0 = 22

    def slots(a, b):
        def one(t):
            if BA:
                band_slot(t)
            if CT:
                pl.when((t >= C0) & (t < C0 + NC + 6 * SKEW))(lambda: corner_slot(t - C0))
        loop(b, one, a)

    def product(k, t=None):
        for half in (0, 1):
            def one(n):
                if MM: piece(k, half, n)
                if t is not None and BA:
                    band_slot(t + 2 * half + n)
                if t is not None and CT:
                    corner_slot(t + 2 * half + n - C0)
            loop(2, one)

    slots(0, 2)
    if CO: corner_part()
    slots(2, 12)
    if BA: own_tile()
    if CO: corner_sum()
    slots(12, C0)
    if CO: corner_take()
    slots(C0, 26)
    product(0, 26)
    if RS: rs_send(0)
    slots(30, 34)
    product(2, 34)
    if RS: rs_send(2)
    if RS: rs_mid(0)
    slots(38, 42)
    product(1, 42)
    if RS:
        rs_send(1)
        rs_mid(2)
        rs_end(0)
    slots(46, T)
    product(3)
    if RS:
        rs_send(3)
        rs_mid(1)
        rs_mid(3)
    if 'f0' in ON: f0_pass()
    if 'f0r' in ON:
        loop(NR + 6 * SKEW, f0r_slot)
        f0r_own()
    if RS:
        for k in (1, 2, 3):
            rs_end(k)

    if BA: band_sent()
    trees_sent()
    if RS:
        for k in range(4):
            rs_sent(k)
    if 'f0' in ON: f0_sent()
    if CO: corner_sent()


def gather(jt, w0, w1, wrow, prior):
    dma = pltpu.SemaphoreType.DMA
    return pl.pallas_call(
        gather_kernel,
        out_shape=[
            jax.ShapeDtypeStruct((2, 512, 512), F32),
            jax.ShapeDtypeStruct((2, 512, 512), BF16),
            jax.ShapeDtypeStruct((512, 512), BF16),
            jax.ShapeDtypeStruct((4, 128, 512), F32),
        ],
        in_specs=[VMEM] * 5,
        out_specs=[VMEM] * 4,
        scratch_shapes=[
            pltpu.VMEM((4, 4 * NCH, CH, 512), BF16),
            pltpu.VMEM((4, 2, 512, 512), BF16),
            pltpu.VMEM((4, 2, 512, 512), BF16),
            pltpu.VMEM((2, 2, 2, 512, 512), BF16),
            pltpu.VMEM((2, 512, 512), F32),
            pltpu.VMEM((4, 128, 512), F32),
            pltpu.VMEM((4, 128, 512), F32),
            pltpu.VMEM((8, 512), F32),
            pltpu.VMEM((4, 8, 512), F32),
            dma((4, 4, 4 * NCH)), dma((4, 4 * NCH)), dma,
            dma((4, 4, NC)), dma((4, NC)), dma((4, 4, NR)), dma((4, NR)),
            dma((4, 2)), dma((4, 2)), dma((2, 2, 2)), dma((2, 2)), dma((2,)),
            dma((2, 3)), dma((2, 4)), dma, dma((4,)),
        ],
        compiler_params=pltpu.CompilerParams(
            collective_id=0, has_side_effects=True, vmem_limit_bytes=58 * 2**20
        ),
        cost_estimate=pl.CostEstimate(flops=2 * 2048 * 2048 * 1024, bytes_accessed=2**24, transcendentals=0),
    )(jt, w0, w1, wrow, prior)


def split3(x):
    a = x.astype(BF16)
    rest = x - a.astype(F32)
    b = rest.astype(BF16)
    return a, b, (rest - b.astype(F32)).astype(BF16)


def invert_tile(m, size=16):
    lane = lax.broadcasted_iota(jnp.int32, (size, 128), 1)
    row = lax.broadcasted_iota(jnp.int32, (size, 128), 0)
    rows = lax.broadcasted_iota(jnp.int32, (128, 128), 0)
    lanes = lax.broadcasted_iota(jnp.int32, (128, 128), 1)
    spread = lambda v: jnp.broadcast_to(v, (size, 128))

    def panel(p, m):
        active = 128 - size * p
        x = m[:size]
        cols = [spread(x[:, j:j + 1]) for j in range(size)]
        pivots = jnp.zeros((size, 128), F32)
        d = spread(cols[0][0:1])
        for j in range(size):
            q = pl.reciprocal(d, approx=True)
            q = q * (2.0 - d * q)
            pivots = jnp.where(row == j, d, pivots)
            below = jnp.where(row > j, cols[j], 0.0)
            if j + 1 < size:
                d = spread(cols[j + 1][j + 1:j + 2]) - q * (
                    spread(cols[j][j + 1:j + 2]) * spread(cols[j + 1][j:j + 1])
                )
            u = spread(jnp.where(lane[:1] == j, 1.0, x[j:j + 1]))
            x = jnp.where((lane == j) & (row >= j), jnp.where(row == j, 1.0, 0.0), x)
            x = x - q * (below * u)
            for k in range(j + 1, size):
                cols[k] = cols[k] - q * (below * spread(cols[k][j:j + 1]))
        s = lax.rsqrt(pivots)
        x = x * (s * (1.5 - 0.5 * pivots * s * s))
        x = jnp.where((lane < size) & (lane > row), 0.0, x)
        left = jnp.where((lane >= size) & (lane < active), x, 0.0)
        x1, x2, x3 = split3(x)
        y1, y2, y3 = split3(left)
        update = dotp(
            jnp.concatenate([y1, y1, y2, y2, y1, y3], axis=0),
            jnp.concatenate([x1, x2, x1, x2, x3, x1], axis=0), 0, 0,
        )
        m = jnp.where((lanes < size) & (rows < active), 0.0, m) - update
        m = jnp.concatenate([m[size:], x], axis=0)
        return pltpu.roll(m, 128 - size, 1)

    m = lax.fori_loop(0, 128 // size, panel, m)
    return jnp.where(rows >= lanes, m, 0.0)


def invert_factor(a):
    for j in range(4):
        here = slice(128 * j, 128 * (j + 1))
        t = invert_tile(a[here, here])
        a[here, here] = t
        if j > 0:
            a[here, 0:128 * j] = dotp(t, a[here, 0:128 * j], precision=HIGHEST)
        if j < 3:
            low = 128 * (j + 1)
            a[here, low:] = dotp(t, a[here, low:], precision=HIGHEST)
            u = a[here, :]
            lanes = lax.broadcasted_iota(jnp.int32, (512 - low, 512), 1)
            kept = jnp.where((lanes >= 128 * j) & (lanes < low), 0.0, a[low:, :])
            a[low:, :] = kept - dotp(u[:, low:], u, 0, 0, precision=HIGHEST)
    a_rows = lax.broadcasted_iota(jnp.int32, (512, 512), 0)
    a_lanes = lax.broadcasted_iota(jnp.int32, (512, 512), 1)
    a[...] = jnp.where(a_rows >= a_lanes, a[...], 0.0)


def dot3(a, b, ca=1, cb=0):
    return dotp(a[0], b[0], ca, cb) + (dotp(a[0], b[1], ca, cb) + dotp(a[1], b[0], ca, cb))


def pair(x):
    a = x.astype(BF16)
    return a, (x - a.astype(F32)).astype(BF16)


def factor_kernel(f, f0, f0r, corner, out, a, res, sem):
    r, c = lax.axis_index("row"), lax.axis_index("col")
    for q in range(4):
        a[128 * q:128 * (q + 1), :] = corner[q]
    invert_factor(a)
    linv = pair(a[...])

    def put(half):
        return pltpu.make_async_copy(res.at[half], out.at[:, half, :], sem.at[half])

    def panel(half):
        return dotp(linv[0], f0[half]) + dotp(linv[1], f0[half])

    @pl.when(r == 0)
    def _():
        @pl.when(c == 0)
        def _():
            res[0] = dot3(linv, pair(corner[...].reshape(512, 512)))

        @pl.when(c != 0)
        def _():
            res[0] = panel(0)
        put(0).start()
        res[1] = panel(1)
        put(1).start()

    @pl.when(r != 0)
    def _():
        right = pair(dotp(linv[0], f0r[...]) + dotp(linv[1], f0r[...]))

        @pl.when(c == 0)
        def _():
            res[0] = f[0]

        @pl.when(c != 0)
        def _():
            res[0] = f[0] - dot3(right, pair(panel(0)), 0, 0)
        put(0).start()
        res[1] = f[1] - dot3(right, pair(panel(1)), 0, 0)
        put(1).start()

    for half in (0, 1):
        put(half).wait()


def factor(f, f0, f0r, corner):
    return pl.pallas_call(
        factor_kernel,
        out_shape=jax.ShapeDtypeStruct((512, 2, 512), F32),
        in_specs=[VMEM] * 4,
        out_specs=pl.BlockSpec(memory_space=pl.ANY),
        scratch_shapes=[
            pltpu.VMEM((512, 512), F32),
            pltpu.VMEM((2, 512, 512), F32),
            pltpu.SemaphoreType.DMA((2,)),
        ],
        compiler_params=pltpu.CompilerParams(vmem_limit_bytes=56 * 2**20),
        cost_estimate=pl.CostEstimate(flops=2**31, bytes_accessed=2**23, transcendentals=0),
    )(f, f0, f0r, corner)


def body(sensitivity, sample_weight, pattern, prior):
    blocks = pattern.shape[0]
    x = sensitivity.reshape(blocks * 512, 1024)
    mask = jnp.repeat(pattern[:, :, 0].astype(F32), 512, axis=0)
    scale = sample_weight[:, None] * mask
    w = [
        (scale[:, i:i + 1] * x[:, 512 * i:512 * (i + 1)].astype(F32)).astype(BF16).reshape(blocks, 512, 512)
        for i in (0, 1)
    ]
    jt = (x[:, :512] * mask[:, 0:1].astype(BF16)).reshape(blocks, 512, 512).transpose(0, 2, 1)
    f, f0, f0r, corner = gather(
        jt, w[0], w[1], sample_weight.reshape(blocks, 1, 512), prior.reshape(1, 512)
    )
    return factor(f, f0, f0r, corner)


def solution(mesh):
    return jax.shard_map(
        body,
        mesh=mesh,
        in_specs=(P("row", None, "col"), P("row"), P("row", None, "col"), P("row")),
        out_specs=P("row", None, "col"),
        check_vma=False,
    )
```

time: 705 us -> 192 us (0.27)
  the two profiles are of different devices: /device:TPU:71 before, /device:TPU:49 now
where the time goes in v1:
time: 192 us
  Pallas kernels  181 us (94%)
  local copies, waits for them, and re-layouts  5.86 us (3%)
  other arithmetic  4.21 us (2%)
    pallas_call x1, Pallas kernels, gather(): pl.pallas_call(gather_kernel, out_shape=[jax.ShapeDtypeStruct((2, 512, 51...  155 us
    pallas_call x1, Pallas kernels, factor(): pl.pallas_call(factor_kernel, out_shape=jax.ShapeDtypeStruct((512, 2, 512...  26.4 us

profile of v1, /device:TPU:49, one launch (start us, length us, event | category | flops | bytes accessed | tf_op | source)
XLA Modules:
  0.0 191.6 jit_solution(4495452243817243206)
XLA Ops:
  0.0 0.7 convert_element_type.19
  0.7 0.1 broadcast_bitcast_fusion
  0.8 0.7 broadcast_multiply_fusion
  1.5 3.4 %copy.7 = bf16[256,8,2,512]{3,1,2,0:T(8,128)(2,1)S(1)} copy(bf16[256,8,2,512]{3,2,1,0:T(2,128)(2,1)} %bitcast.19) | data formatting | bytes 8388608
  4.9 0.3 slice_multiply_fusion
  5.3 2.5 %multiply_convert_fusion = (bf16[2048,512]{1,0:T(8,128)(2,1)}, bf16[2048,512]{1,0:T(8,128)(2,1)}) fusion(bf16[2048,1024]{1,0:T(8,128)(2,1)S(1)} %bitcast.17, f32[2048]{0:T(1024)S(1)} %bitcast.25, f32[2048]{0:T(1024)S(1)} %bitcast.26), kind=kLoop, calls=%fused_computation | loop fusion | flops 6291456 | bytes 8404992 | tf_op jit(solution)/shard_map/convert_element_type | solution.py:671
  7.7 2.4 %copy.6 = bf16[4,512,512]{1,2,0:T(8,128)(2,1)} copy(bf16[4,512,512]{2,1,0:T(8,128)(2,1)S(1)} %bitcast.18) | data formatting | bytes 4194304 | tf_op jit(solution)/shard_map/reshape | solution.py:674
  10.1 154.8 %shard_map.46 = (f32[2,512,512]{2,1,0:T(8,128)}, bf16[2,512,512]{2,1,0:T(8,128)(2,1)}, bf16[512,512]{1,0:T(8,128)(2,1)}, f32[4,128,512]{2,1,0:T(8,128)}) custom-call(bf16[4,512,512]{2,1,0:T(8,128)(2,1)} %bitcast.20, bf16[4,512,512]{2,1,0:T(8,128)(2,1)} %bitcast.22, bf16[4,512,512]{2,1,0:T(8,128)(2,1)} %bitcast.21, f32[4,1,512]{2,1,0:T(1,128)} %bitcast.27, ...), custom_call_target="tpu_custom_call" | custom-call | flops 8589934592 | bytes 16777216 | tf_op jit(solution)/shard_map/pallas_call | solution.py:492
  165.0 26.4 %shard_map.47 = f32[512,2,512]{2,1,0:T(2,128)} custom-call(f32[2,512,512]{2,1,0:T(8,128)} %get-tuple-element.9.f, bf16[2,512,512]{2,1,0:T(8,128)(2,1)} %get-tuple-element.10.f0, bf16[512,512]{1,0:T(8,128)(2,1)} %get-tuple-element.11.f0r, f32[4,128,512]{2,1,0:T(8,128)} %get-tuple-element.12.corner), custom_call_target="tpu_custom_call" | custom-call | flops 2147483648 | bytes 8388608 | tf_op jit(solution)/shard_map/pallas_call | solution.py:650
  (3 shorter events, 0.1 us)

commit v2 on v1

--- a/solution.py
+++ b/solution.py
@@ -12,10 +12,10 @@
 VMEM = pl.BlockSpec(memory_space=pltpu.VMEM)
 NCH = 8
 CH = 512 // NCH
-SKEW = 3
-ON = {'band', 'corner', 'mm', 'rs', 'f0', 'f0r', 'ctree'}
+SKEW = 4
 TILES = (0, 2, 1, 3)
-T = 4 * NCH + 6 * SKEW
+T = 4 * NCH + 5 * SKEW
+SKEWR = 4
 NC = 4
 NR = 2
 SEND = {
@@ -60,21 +60,23 @@
 
 
 class Tree:
-    def __init__(self, pos, q, sy):
+    def __init__(self, pos, m, sy, skew):
         dz, dy = pos.z, (pos.y - sy + 4) % 4
         mz, my = (4 - dz) % 4, (4 - dy) % 4
-        u, v = ((dz, dy), (dy, mz), (mz, my), (my, dz))[q]
-        fwd = ((0, 1), (3, 0), (0, 3), (1, 0))[q]
-        side = ((1, 0), (0, 1), (3, 0), (0, 3))[q]
+        first = pos.core == 0
+        pick = lambda table: tuple(
+            jnp.where(first, a, b) for a, b in zip(table[m], table[2 + m])
+        )
+        u, v = pick(((dz, dy), (dy, mz), (mz, my), (my, dz)))
+        fwd = pick(((0, 1), (3, 0), (0, 3), (1, 0)))
+        side = pick(((1, 0), (0, 1), (3, 0), (0, 3)))
         back = tuple((4 - d) % 4 for d in fwd)
         other = tuple((4 - d) % 4 for d in side)
-        des = q // 2
-        to = lambda d: pos.at((pos.z + d[0]) % 4, (pos.y + d[1]) % 4, des)
+        to = lambda d: pos.at((pos.z + d[0]) % 4, (pos.y + d[1]) % 4, pos.core)
+        self.q = 2 * pos.core + m
         self.at_source = (dz == 0) & (dy == 0)
-        self.holder = jnp.logical_not(self.at_source) & (pos.core == des)
         depth = jnp.where(u == 0, v, 2 + jnp.where(u == 2, 1, 0) + jnp.where(v == 0, 1, v - 1))
-        depth = jnp.where(pos.core == des, depth, depth + 1)
-        self.start = SKEW * jnp.where(self.at_source, 1, depth)
+        self.start = jnp.where(self.at_source, -1000, skew * depth)
         ahead = ((u == 0) & (v < 3)) | ((u >= 1) & ((v == 1) | (v == 2)))
         turn = tuple(jnp.where(u == 0, a, b) for a, b in zip(side, back))
         self.children = (
@@ -82,36 +84,92 @@
             (v == 1, to(turn)),
             ((v == 1) & ((u == 0) | (u == 3)), to(other)),
         )
-        self.root_child = to(fwd)
-        self.sib = pos.sib
-
-
-def copies_of(tree, src, dst, send, recv, idx):
-    out = []
-    for n, (pred, to) in enumerate(tree.children + ((True, tree.sib),)):
-        out.append((pred, pltpu.make_async_remote_copy(
-            src, dst, send.at[(n,) + idx], recv.at[idx], device_id=to, device_id_type=MESH
-        )))
-    return out
-
-
-def pass_on(tree, copies, do):
-    @pl.when(tree.holder)
-    def _():
-        for pred, copy in copies[:3]:
-            pl.when(pred)(getattr(copy, do))
-        getattr(copies[3][1], do)()
-
-
-def set_out(tree, copies, do):
-    getattr(copies[0][1], do)()
-    getattr(copies[3][1], do)()
+
+
+class Spread:
+    def __init__(self, pos, sy, column, n, src, dst, send, recv, sib_send, sib_recv, skew=SKEW):
+        self.pos, self.column, self.n = pos, column, n
+        self.trees = [Tree(pos, m, sy, skew) for m in (0, 1)]
+        self.dst, self.send, self.recv = dst, send, recv
+        self.sib_send, self.sib_recv = sib_send, sib_recv
+        self.src = src
+        self.mine = pos.col == column
+        self.sy = sy
+
+    def children(self, tree, i):
+        q = tree.q
+        return [
+            (pred, pltpu.make_async_remote_copy(
+                self.dst(q, i, 1), self.dst(q, i, 1), self.send.at[k, q, i], self.recv.at[q, i],
+                device_id=to, device_id_type=MESH))
+            for k, (pred, to) in enumerate(tree.children)
+        ]
+
+    def root(self, q, i):
+        step = ((0, 1), (3, 0), (0, 3), (1, 0))[q]
+        pos = self.pos
+        return pltpu.make_async_remote_copy(
+            self.src(q, i, 1), self.dst(q, i, 1), self.send.at[0, q, i], self.recv.at[q, i],
+            device_id=pos.at(step[0], (self.sy + step[1]) % 4, q // 2), device_id_type=MESH)
+
+    def sibling(self, q, src):
+        return pltpu.make_async_remote_copy(
+            src(q, 0, self.n), self.dst(q, 0, self.n), self.sib_send.at[q], self.sib_recv.at[q],
+            device_id=self.pos.sib, device_id_type=MESH)
+
+    def begin(self, t):
+        @pl.when(self.mine & (t >= 0) & (t < self.n))
+        def _():
+            for q in range(4):
+                self.root(q, t).start()
+
+            @pl.when(t == self.n - 1)
+            def _():
+                for q in range(4):
+                    self.sibling(q, self.src).start()
+
+    def slot(self, t):
+        self.begin(t)
+        for tree in self.trees:
+            i = t - tree.start
+
+            @pl.when((i >= 0) & (i < self.n))
+            def _():
+                copies = self.children(tree, i)
+                copies[0][1].wait_recv()
+                for pred, copy in copies:
+                    pl.when(pred)(copy.start)
+                pl.when(i == self.n - 1)(lambda: self.sibling(tree.q, self.dst).start())
+
+    def take(self):
+        away = jnp.logical_not(self.trees[0].at_source)
+        other = 1 - self.pos.core
+        for q in range(4):
+            @pl.when((away & (other == q // 2)) | (self.trees[0].at_source & jnp.logical_not(self.mine)))
+            def _():
+                self.sibling(q, self.dst).wait_recv()
+
+    def sent(self):
+        @pl.when(self.mine)
+        def _():
+            for q in range(4):
+                loop(self.n, lambda i: self.root(q, i).wait_send())
+                self.sibling(q, self.src).wait_send()
+        for tree in self.trees:
+            @pl.when(jnp.logical_not(tree.at_source))
+            def _():
+                def one(i):
+                    for pred, copy in self.children(tree, i):
+                        pl.when(pred)(copy.wait_send)
+                loop(self.n, one)
+                self.sibling(tree.q, self.dst).wait_send()
 
 
 def gather_kernel(
-    jt, w0, w1, wrow, prior, f_out, f0_out, f0r_out, corner,
+    jt, w0, w1, wrow, prior, f_out, f0_out, f0r_out, corner, linv,
     band, pb, rxm, rxd, f0acc, cpart, crx, dg, dgr,
-    b_send, b_recv, own_sem, c_send, c_recv, r_send, r_recv,
+    b_send, b_recv, bs_send, bs_recv, c_send, c_recv, cs_send, cs_recv,
+    r_send, r_recv, rs_send2, rs_recv2,
     rs_sem, rxm_sem, rxd_sem, f0_send, f0_recv, cx_send, cx_recv, dg_send, dg_recv,
 ):
     pos = Place()
@@ -127,50 +185,47 @@
         pl.semaphore_signal(barrier, inc=1, device_id=to, device_id_type=MESH)
     pl.semaphore_wait(barrier, len(greet))
 
-    chips = [[Tree(pos, q, sy) for q in range(4)] for sy in (0, 1)]
-
-    def band_copies(tree, q, i, own=None):
-        src = band.at[q, i] if own is None else jt.at[q, pl.ds(pl.multiple_of(own * CH, CH), CH)]
-        return copies_of(tree, src, band.at[q, i], b_send, b_recv, (q, i))
+    def run(q, i, n, rows):
+        return pl.ds(pl.multiple_of((q * 0 + i) * rows, rows), n * rows)
+
+    bands = []
+    for n, tile in enumerate(TILES):
+        bands.append(Spread(
+            pos, tile // 2, tile, NCH,
+            lambda q, i, m: jt.at[q, run(q, i, m, CH)],
+            lambda q, i, m, n=n: band.at[q, n, run(q, i, m, CH)],
+            b_send.at[n], b_recv.at[n], bs_send.at[n], bs_recv.at[n]))
+
+    def corner_rows(q, i, m):
+        return corner.at[q, run(q, i, m, 128 // NC)]
+
+    corners = Spread(pos, 0, 0, NC, corner_rows, corner_rows, c_send, c_recv, cs_send, cs_recv)
+
+    def f0r_rows(ref):
+        return lambda q, i, m: ref.at[pl.ds(
+            pl.multiple_of(q * 128 + i * (128 // NR), 128 // NR), m * (128 // NR))]
+
+    f0rs = Spread(pos, r // 2, r, NR, f0r_rows(f0_out.at[0]), f0r_rows(f0r_out),
+                  r_send, r_recv, rs_send2, rs_recv2, SKEWR)
 
     def band_slot(t):
-        for n, tile in enumerate(TILES):
-            @pl.when((c == tile) & (t >= NCH * n) & (t < NCH * (n + 1)))
-            def _():
-                for q in range(4):
-                    tree = chips[tile // 2][q]
-                    set_out(tree, band_copies(tree, q, t, t - NCH * n), "start")
-        for sy in (0, 1):
-            for q in range(4):
-                tree = chips[sy][q]
-                i = t - tree.start - NCH * sy
-
-                @pl.when((i >= 0) & (i < 3 * NCH) & ((i < NCH) | (i >= 2 * NCH)))
-                def _():
-                    @pl.when(c != 2 * sy + jnp.where(i < NCH, 0, 1))
-                    def _():
-                        copies = band_copies(tree, q, i + NCH * sy)
-                        copies[3][1].wait_recv()
-                        pass_on(tree, copies, "start")
-
-    def band_sent():
-        for n, tile in enumerate(TILES):
-            for q in range(4):
-                tree = chips[tile // 2][q]
-
-                def done(ch):
-                    copies = band_copies(tree, q, NCH * n + ch)
-                    pl.when(c == tile)(lambda: set_out(tree, copies, "wait_send"))
-                    pass_on(tree, copies, "wait_send")
-                loop(NCH, done)
+        for n in range(4):
+            @pl.when((t >= NCH * n) & (t < NCH * (n + 1) + 5 * SKEW))
+            def _():
+                bands[n].slot(t - NCH * n)
+
+    def corner_slot(t):
+        corners.slot(t)
+
+    def f0r_slot(t):
+        f0rs.slot(t)
 
     def own_tile():
         for n, tile in enumerate(TILES):
             @pl.when(c == tile)
             def _():
                 for q in range(4):
-                    for ch in range(NCH):
-                        band[q, NCH * n + ch] = jt[q, CH * ch:CH * (ch + 1)]
+                    band[q, n] = jt[q]
 
     def corner_x(dst, src, i, kind, frm):
         return pltpu.make_async_remote_copy(
@@ -217,67 +272,13 @@
                 corner_x(crx.at[r], cpart.at[(r + i) % 4], i, 0, r).wait_send()
                 corner_x(corner.at[r], corner.at[r], i, 1, r).wait_send()
 
-    def corner_copies(q, ch):
-        n = 128 // NC
-        ref = corner.at[q, pl.ds(pl.multiple_of(ch * n, n), n)]
-        return copies_of(chips[0][q], ref, ref, c_send, c_recv, (q, ch))
-
-    def corner_slot(t):
-        @pl.when((c == 0) & (t < NC))
-        def _():
-            for q in range(4):
-                set_out(chips[0][q], corner_copies(q, t), "start")
-        for q in range(4):
-            i = t - chips[0][q].start
-
-            @pl.when((c != 0) & (i >= 0) & (i < NC))
-            def _():
-                copies = corner_copies(q, i)
-                copies[3][1].wait_recv()
-                pass_on(chips[0][q], copies, "start")
-
-    rtrees = [Tree(pos, q, r // 2) for q in range(4)]
-
-    def f0r_copies(q, ch, own=False):
-        n = 128 // NR
-        rows = pl.ds(pl.multiple_of(q * 128 + ch * n, n), n)
-        src = f0_out.at[0, rows] if own else f0r_out.at[rows]
-        return copies_of(rtrees[q], src, f0r_out.at[rows], r_send, r_recv, (q, ch))
-
-    def f0r_slot(t):
-        @pl.when((c == r) & (t < NR))
-        def _():
-            for q in range(4):
-                set_out(rtrees[q], f0r_copies(q, t, True), "start")
-        for q in range(4):
-            i = t - rtrees[q].start
-
-            @pl.when((c != r) & (i >= 0) & (i < NR))
-            def _():
-                copies = f0r_copies(q, i)
-                copies[3][1].wait_recv()
-                pass_on(rtrees[q], copies, "start")
-
     def f0r_own():
         @pl.when(c == r)
         def _():
             f0r_out[...] = f0_out[0]
 
-    def trees_sent():
-        for q in range(4):
-            for n, at, tree, copies in (
-                (NC, 0, chips[0][q], corner_copies), (NR, r, rtrees[q], f0r_copies),
-            ):
-                if ('ctree' if n == NC else 'f0r') not in ON:
-                    continue
-                for ch in range(n):
-                    cp = copies(q, ch)
-                    pl.when(c == at)(lambda: set_out(tree, cp, "wait_send"))
-                    pl.when(c != at)(lambda: pass_on(tree, cp, "wait_send"))
-
     def tile_of(k, q):
-        n = TILES.index(k)
-        return band[q, NCH * n:NCH * (n + 1)].reshape(512, 512)
+        return band[q, TILES.index(k)]
 
     def piece(k, half, n):
         cols = pl.ds(pl.multiple_of(n * 256, 256), 256)
@@ -306,10 +307,10 @@
         @pl.when(c == 0)
         def _():
             value = acc
-            first = pl.ds(pl.multiple_of(n * (NCH // 2), NCH // 2), NCH // 2)
+            first = pl.ds(pl.multiple_of(n * 256, 256), 256)
             for q in range(4):
                 wk = (tile_of(k, q).astype(F32) * wrow[q]).astype(BF16)
-                value = value - dotp(wk, band[q, first].reshape(256, 512), 1, 1)
+                value = value - dotp(wk, band[q, 0, first], 1, 1)
             put(value)
 
         @pl.when(c == k)
@@ -370,7 +371,7 @@
                 if k == 0:
                     f0_out[half] = (f0acc[half] + got).astype(BF16)
                     for step in (1, 3):
-                        if 'f0' in ON: f0_copy(half, step).start()
+                        f0_copy(half, step).start()
                 else:
                     f_out[half] = f_out[half] + got
             if k == 0:
@@ -406,13 +407,13 @@
             device_id=pos.along(step), device_id_type=MESH,
         )
 
-    def f0_pass():
-        @pl.when(r != 2)
-        def _():
-            for half in (0, 1):
-                f0_copy(half, 1).wait_recv()
-        pl.when(r == 1)(f0_copy(0, 3).start)
-        pl.when(r == 3)(f0_copy(1, 1).start)
+    def f0_take(half, rows):
+        for row in rows:
+            pl.when(r == row)(f0_copy(half, 1).wait_recv)
+        if half == 0:
+            if 1 in rows: pl.when(r == 1)(f0_copy(0, 3).start)
+        elif 3 in rows:
+            pl.when(r == 3)(f0_copy(1, 1).start)
 
     def f0_sent():
         @pl.when(r == 2)
@@ -423,68 +424,77 @@
         pl.when(r == 1)(f0_copy(0, 3).wait_send)
         pl.when(r == 3)(f0_copy(1, 1).wait_send)
 
-    RS, MM, BA, CO, CT = ('rs' in ON), ('mm' in ON), ('band' in ON), ('corner' in ON), ('ctree' in ON)
-    C0 = 22
+    C0 = 20
+
+    def both(t):
+        band_slot(t)
+        pl.when((t >= C0) & (t < C0 + NC + 5 * SKEW))(lambda: corner_slot(t - C0))
 
     def slots(a, b):
-        def one(t):
-            if BA:
-                band_slot(t)
-            if CT:
-                pl.when((t >= C0) & (t < C0 + NC + 6 * SKEW))(lambda: corner_slot(t - C0))
-        loop(b, one, a)
+        loop(b, both, a)
 
     def product(k, t=None):
+        bands[TILES.index(k)].take()
         for half in (0, 1):
             def one(n):
-                if MM: piece(k, half, n)
-                if t is not None and BA:
-                    band_slot(t + 2 * half + n)
-                if t is not None and CT:
-                    corner_slot(t + 2 * half + n - C0)
+                piece(k, half, n)
+                if t is not None: both(t + 2 * half + n)
             loop(2, one)
 
     slots(0, 2)
-    if CO: corner_part()
+    corner_part()
     slots(2, 12)
-    if BA: own_tile()
-    if CO: corner_sum()
+    own_tile()
+    corner_sum()
     slots(12, C0)
-    if CO: corner_take()
-    slots(C0, 26)
-    product(0, 26)
-    if RS: rs_send(0)
-    slots(30, 34)
-    product(2, 34)
-    if RS: rs_send(2)
-    if RS: rs_mid(0)
-    slots(38, 42)
-    product(1, 42)
-    if RS:
-        rs_send(1)
-        rs_mid(2)
-        rs_end(0)
-    slots(46, T)
+    corner_take()
+    P0 = NCH + 5 * SKEW
+    slots(C0, P0 + 1)
+    product(0, P0 + 1)
+    rs_send(0)
+    slots(P0 + 5, P0 + NCH + 1)
+    product(2, P0 + NCH + 1)
+    rs_send(2)
+    rs_mid(0)
+    slots(P0 + NCH + 5, P0 + 2 * NCH + 1)
+    product(1, P0 + 2 * NCH + 1)
+    rs_send(1)
+    rs_mid(2)
+    rs_end(0)
+    slots(P0 + 2 * NCH + 5, T)
     product(3)
-    if RS:
-        rs_send(3)
-        rs_mid(1)
-        rs_mid(3)
-    if 'f0' in ON: f0_pass()
-    if 'f0r' in ON:
-        loop(NR + 6 * SKEW, f0r_slot)
+    corners.take()
+    rs_send(3)
+    rs_mid(1)
+    for q in range(4):
+        linv[128 * q:128 * (q + 1), :] = corner[q]
+    beside = lambda j: lambda p: pl.when(r != 0)(lambda: f0r_slot(p + 8 * j))
+    invert_step(linv, 0)
+    rs_mid(3)
+    invert_step(linv, 1)
+    f0_take(0, (1, 3))
+    invert_step(linv, 2, beside(0))
+    f0_take(1, (1, 3))
+    invert_step(linv, 3, beside(1))
+
+    @pl.when(r != 0)
+    def _():
+        loop(NR + 5 * SKEWR, f0r_slot, 16)
         f0r_own()
-    if RS:
-        for k in (1, 2, 3):
-            rs_end(k)
-
-    if BA: band_sent()
-    trees_sent()
-    if RS:
-        for k in range(4):
-            rs_sent(k)
-    if 'f0' in ON: f0_sent()
-    if CO: corner_sent()
+        f0rs.take()
+
+    f0_take(0, (0,))
+    f0_take(1, (0,))
+    for k in (1, 2, 3):
+        rs_end(k)
+
+    for spread in bands: spread.sent()
+    corners.sent()
+    pl.when(r != 0)(f0rs.sent)
+    for k in range(4):
+        rs_sent(k)
+    f0_sent()
+    corner_sent()
 
 
 def gather(jt, w0, w1, wrow, prior):
@@ -496,11 +506,12 @@
             jax.ShapeDtypeStruct((2, 512, 512), BF16),
             jax.ShapeDtypeStruct((512, 512), BF16),
             jax.ShapeDtypeStruct((4, 128, 512), F32),
+            jax.ShapeDtypeStruct((512, 512), F32),
         ],
         in_specs=[VMEM] * 5,
-        out_specs=[VMEM] * 4,
+        out_specs=[VMEM] * 5,
         scratch_shapes=[
-            pltpu.VMEM((4, 4 * NCH, CH, 512), BF16),
+            pltpu.VMEM((4, 4, 512, 512), BF16),
             pltpu.VMEM((4, 2, 512, 512), BF16),
             pltpu.VMEM((4, 2, 512, 512), BF16),
             pltpu.VMEM((2, 2, 2, 512, 512), BF16),
@@ -509,8 +520,9 @@
             pltpu.VMEM((4, 128, 512), F32),
             pltpu.VMEM((8, 512), F32),
             pltpu.VMEM((4, 8, 512), F32),
-            dma((4, 4, 4 * NCH)), dma((4, 4 * NCH)), dma,
-            dma((4, 4, NC)), dma((4, NC)), dma((4, 4, NR)), dma((4, NR)),
+            dma((4, 3, 4, NCH)), dma((4, 4, NCH)), dma((4, 4)), dma((4, 4)),
+            dma((3, 4, NC)), dma((4, NC)), dma((4,)), dma((4,)),
+            dma((3, 4, NR)), dma((4, NR)), dma((4,)), dma((4,)),
             dma((4, 2)), dma((4, 2)), dma((2, 2, 2)), dma((2, 2)), dma((2,)),
             dma((2, 3)), dma((2, 4)), dma, dma((4,)),
         ],
@@ -528,7 +540,7 @@
     return a, b, (rest - b.astype(F32)).astype(BF16)
 
 
-def invert_tile(m, size=16):
+def invert_tile(m, size=16, beside=None):
     lane = lax.broadcasted_iota(jnp.int32, (size, 128), 1)
     row = lax.broadcasted_iota(jnp.int32, (size, 128), 0)
     rows = lax.broadcasted_iota(jnp.int32, (128, 128), 0)
@@ -536,6 +548,8 @@
     spread = lambda v: jnp.broadcast_to(v, (size, 128))
 
     def panel(p, m):
+        if beside is not None:
+            beside(p)
         active = 128 - size * p
         x = m[:size]
         cols = [spread(x[:, j:j + 1]) for j in range(size)]
@@ -573,23 +587,23 @@
     return jnp.where(rows >= lanes, m, 0.0)
 
 
-def invert_factor(a):
-    for j in range(4):
-        here = slice(128 * j, 128 * (j + 1))
-        t = invert_tile(a[here, here])
-        a[here, here] = t
-        if j > 0:
-            a[here, 0:128 * j] = dotp(t, a[here, 0:128 * j], precision=HIGHEST)
-        if j < 3:
-            low = 128 * (j + 1)
-            a[here, low:] = dotp(t, a[here, low:], precision=HIGHEST)
-            u = a[here, :]
-            lanes = lax.broadcasted_iota(jnp.int32, (512 - low, 512), 1)
-            kept = jnp.where((lanes >= 128 * j) & (lanes < low), 0.0, a[low:, :])
-            a[low:, :] = kept - dotp(u[:, low:], u, 0, 0, precision=HIGHEST)
-    a_rows = lax.broadcasted_iota(jnp.int32, (512, 512), 0)
-    a_lanes = lax.broadcasted_iota(jnp.int32, (512, 512), 1)
-    a[...] = jnp.where(a_rows >= a_lanes, a[...], 0.0)
+def invert_step(a, j, beside=None):
+    here = slice(128 * j, 128 * (j + 1))
+    t = invert_tile(a[here, here], beside=beside)
+    a[here, here] = t
+    if j > 0:
+        a[here, 0:128 * j] = dotp(t, a[here, 0:128 * j], precision=HIGHEST)
+    if j < 3:
+        low = 128 * (j + 1)
+        a[here, low:] = dotp(t, a[here, low:], precision=HIGHEST)
+        u = a[here, :]
+        lanes = lax.broadcasted_iota(jnp.int32, (512 - low, 512), 1)
+        kept = jnp.where((lanes >= 128 * j) & (lanes < low), 0.0, a[low:, :])
+        a[low:, :] = kept - dotp(u[:, low:], u, 0, 0, precision=HIGHEST)
+    else:
+        rows = lax.broadcasted_iota(jnp.int32, (512, 512), 0)
+        lanes = lax.broadcasted_iota(jnp.int32, (512, 512), 1)
+        a[...] = jnp.where(rows >= lanes, a[...], 0.0)
 
 
 def dot3(a, b, ca=1, cb=0):
@@ -601,12 +615,9 @@
     return a, (x - a.astype(F32)).astype(BF16)
 
 
-def factor_kernel(f, f0, f0r, corner, out, a, res, sem):
+def finish_kernel(f, f0, f0r, corner, inverse, out, res, sem):
     r, c = lax.axis_index("row"), lax.axis_index("col")
-    for q in range(4):
-        a[128 * q:128 * (q + 1), :] = corner[q]
-    invert_factor(a)
-    linv = pair(a[...])
+    linv = pair(inverse[...])
 
     def put(half):
         return pltpu.make_async_copy(res.at[half], out.at[:, half, :], sem.at[half])
@@ -646,20 +657,19 @@
         put(half).wait()
 
 
-def factor(f, f0, f0r, corner):
+def finish(f, f0, f0r, corner, inverse):
     return pl.pallas_call(
-        factor_kernel,
+        finish_kernel,
         out_shape=jax.ShapeDtypeStruct((512, 2, 512), F32),
-        in_specs=[VMEM] * 4,
+        in_specs=[VMEM] * 5,
         out_specs=pl.BlockSpec(memory_space=pl.ANY),
         scratch_shapes=[
-            pltpu.VMEM((512, 512), F32),
             pltpu.VMEM((2, 512, 512), F32),
             pltpu.SemaphoreType.DMA((2,)),
         ],
         compiler_params=pltpu.CompilerParams(vmem_limit_bytes=56 * 2**20),
         cost_estimate=pl.CostEstimate(flops=2**31, bytes_accessed=2**23, transcendentals=0),
-    )(f, f0, f0r, corner)
+    )(f, f0, f0r, corner, inverse)
 
 
 def body(sensitivity, sample_weight, pattern, prior):
@@ -672,10 +682,10 @@
         for i in (0, 1)
     ]
     jt = (x[:, :512] * mask[:, 0:1].astype(BF16)).reshape(blocks, 512, 512).transpose(0, 2, 1)
-    f, f0, f0r, corner = gather(
+    f, f0, f0r, corner, inverse = gather(
         jt, w[0], w[1], sample_weight.reshape(blocks, 1, 512), prior.reshape(1, 512)
     )
-    return factor(f, f0, f0r, corner)
+    return finish(f, f0, f0r, corner, inverse)
 
 
 def solution(mesh):

time: 192 us -> 157 us (0.82)
  the two profiles are of different devices: /device:TPU:49 before, /device:TPU:71 now
where the time goes in v2:
time: 157 us; the launch traced here: 156 us
  Pallas kernels  146 us (93%)
  local copies, waits for them, and re-layouts  5.86 us (4%)
  other arithmetic  4.21 us (3%)
    pallas_call x1, Pallas kernels, gather(): pl.pallas_call(gather_kernel, out_shape=[jax.ShapeDtypeStruct((2, 512, 51...  138 us
    pallas_call x1, Pallas kernels, finish(): pl.pallas_call(finish_kernel, out_shape=jax.ShapeDtypeStruct((512, 2, 512...  8.04 us
    unnamed x3, local copies, waits for them, and re-layouts  3.46 us

profile of v2, /device:TPU:71, one launch (start us, length us, event | category | flops | bytes accessed | tf_op | source)
XLA Modules:
  0.0 156.4 jit_solution(16978516862023320290)
XLA Ops:
  0.0 0.7 convert_element_type.19
  0.7 0.1 broadcast_bitcast_fusion
  0.8 0.7 broadcast_multiply_fusion
  1.5 3.4 %copy.7 = bf16[256,8,2,512]{3,1,2,0:T(8,128)(2,1)S(1)} copy(bf16[256,8,2,512]{3,2,1,0:T(2,128)(2,1)} %bitcast.19) | data formatting | bytes 8388608
  4.9 0.3 slice_multiply_fusion
  5.3 2.5 %multiply_convert_fusion = (bf16[2048,512]{1,0:T(8,128)(2,1)}, bf16[2048,512]{1,0:T(8,128)(2,1)}) fusion(bf16[2048,1024]{1,0:T(8,128)(2,1)S(1)} %bitcast.17, f32[2048]{0:T(1024)S(1)} %bitcast.25, f32[2048]{0:T(1024)S(1)} %bitcast.26), kind=kLoop, calls=%fused_computation | loop fusion | flops 6291456 | bytes 8404992 | tf_op jit(solution)/shard_map/convert_element_type | solution.py:681
  7.7 2.4 %copy.6 = bf16[4,512,512]{1,2,0:T(8,128)(2,1)} copy(bf16[4,512,512]{2,1,0:T(8,128)(2,1)S(1)} %bitcast.18) | data formatting | bytes 4194304 | tf_op jit(solution)/shard_map/reshape | solution.py:684
  10.1 138.0 %shard_map.46 = (f32[2,512,512]{2,1,0:T(8,128)}, bf16[2,512,512]{2,1,0:T(8,128)(2,1)}, bf16[512,512]{1,0:T(8,128)(2,1)}, f32[4,128,512]{2,1,0:T(8,128)}, f32[512,512]{1,0:T(8,128)}) custom-call(bf16[4,512,512]{2,1,0:T(8,128)(2,1)} %bitcast.20, bf16[4,512,512]{2,1,0:T(8,128)(2,1)} %bitcast.22, bf16[4,512,512]{2,1,0:T(8,128)(2,1)} %bitcast.21, ...), custom_call_target="tpu_custom_call" | custom-call | flops 8589934592 | bytes 16777216 | tf_op jit(solution)/shard_map/pallas_call | solution.py:502
  148.1 8.0 %shard_map.47 = f32[512,2,512]{2,1,0:T(2,128)} custom-call(f32[2,512,512]{2,1,0:T(8,128)} %get-tuple-element.10.f, bf16[2,512,512]{2,1,0:T(8,128)(2,1)} %get-tuple-element.11.f0, bf16[512,512]{1,0:T(8,128)(2,1)} %get-tuple-element.12.f0r, f32[4,128,512]{2,1,0:T(8,128)} %get-tuple-element.13.corner, f32[512,512]{1,0:T(8,128)} %get-tuple-element.14.inverse), custom_call_target="tpu_custom_call" | custom-call | flops 2147483648 | bytes 8388608 | tf_op jit(solution)/shard_map/pallas_call | solution.py:661
  (3 shorter events, 0.1 us)

commit v3 on v2

--- a/solution.py
+++ b/solution.py
@@ -455,13 +455,13 @@
     slots(P0 + 5, P0 + NCH + 1)
     product(2, P0 + NCH + 1)
     rs_send(2)
-    rs_mid(0)
     slots(P0 + NCH + 5, P0 + 2 * NCH + 1)
     product(1, P0 + 2 * NCH + 1)
     rs_send(1)
+    rs_mid(0)
+    slots(P0 + 2 * NCH + 5, T)
     rs_mid(2)
     rs_end(0)
-    slots(P0 + 2 * NCH + 5, T)
     product(3)
     corners.take()
     rs_send(3)

time: 157 us -> 156 us (level)
  no operation moved by 1% of the time
where the time goes in v3:
time: 156 us; the launch traced here: 155 us
  Pallas kernels  145 us (93%)
  local copies, waits for them, and re-layouts  5.86 us (4%)
  other arithmetic  4.21 us (3%)
    pallas_call x1, Pallas kernels, gather(): pl.pallas_call(gather_kernel, out_shape=[jax.ShapeDtypeStruct((2, 512, 51...  137 us
    pallas_call x1, Pallas kernels, finish(): pl.pallas_call(finish_kernel, out_shape=jax.ShapeDtypeStruct((512, 2, 512...  8.04 us
    unnamed x3, local copies, waits for them, and re-layouts  3.46 us

profile of v3, /device:TPU:71, one launch (start us, length us, event | category | flops | bytes accessed | tf_op | source)
XLA Modules:
  0.0 155.4 jit_solution(6557817314342380746)
XLA Ops:
  0.0 0.7 convert_element_type.19
  0.7 0.1 broadcast_bitcast_fusion
  0.8 0.7 broadcast_multiply_fusion
  1.5 3.4 %copy.7 = bf16[256,8,2,512]{3,1,2,0:T(8,128)(2,1)S(1)} copy(bf16[256,8,2,512]{3,2,1,0:T(2,128)(2,1)} %bitcast.19) | data formatting | bytes 8388608
  4.9 0.3 slice_multiply_fusion
  5.3 2.5 %multiply_convert_fusion = (bf16[2048,512]{1,0:T(8,128)(2,1)}, bf16[2048,512]{1,0:T(8,128)(2,1)}) fusion(bf16[2048,1024]{1,0:T(8,128)(2,1)S(1)} %bitcast.17, f32[2048]{0:T(1024)S(1)} %bitcast.25, f32[2048]{0:T(1024)S(1)} %bitcast.26), kind=kLoop, calls=%fused_computation | loop fusion | flops 6291456 | bytes 8404992 | tf_op jit(solution)/shard_map/convert_element_type | solution.py:681
  7.7 2.4 %copy.6 = bf16[4,512,512]{1,2,0:T(8,128)(2,1)} copy(bf16[4,512,512]{2,1,0:T(8,128)(2,1)S(1)} %bitcast.18) | data formatting | bytes 4194304 | tf_op jit(solution)/shard_map/reshape | solution.py:684
  10.1 137.0 %shard_map.46 = (f32[2,512,512]{2,1,0:T(8,128)}, bf16[2,512,512]{2,1,0:T(8,128)(2,1)}, bf16[512,512]{1,0:T(8,128)(2,1)}, f32[4,128,512]{2,1,0:T(8,128)}, f32[512,512]{1,0:T(8,128)}) custom-call(bf16[4,512,512]{2,1,0:T(8,128)(2,1)} %bitcast.20, bf16[4,512,512]{2,1,0:T(8,128)(2,1)} %bitcast.22, bf16[4,512,512]{2,1,0:T(8,128)(2,1)} %bitcast.21, ...), custom_call_target="tpu_custom_call" | custom-call | flops 8589934592 | bytes 16777216 | tf_op jit(solution)/shard_map/pallas_call | solution.py:502
  147.1 8.0 %shard_map.47 = f32[512,2,512]{2,1,0:T(2,128)} custom-call(f32[2,512,512]{2,1,0:T(8,128)} %get-tuple-element.10.f, bf16[2,512,512]{2,1,0:T(8,128)(2,1)} %get-tuple-element.11.f0, bf16[512,512]{1,0:T(8,128)(2,1)} %get-tuple-element.12.f0r, f32[4,128,512]{2,1,0:T(8,128)} %get-tuple-element.13.corner, f32[512,512]{1,0:T(8,128)} %get-tuple-element.14.inverse), custom_call_target="tpu_custom_call" | custom-call | flops 2147483648 | bytes 8388608 | tf_op jit(solution)/shard_map/pallas_call | solution.py:661
  (3 shorter events, 0.1 us)
